TPU v7x, 128 devices: a whole 4x4x4 slice. The times are simulated.
128 devices in a mesh: group: 8 (over z, core), local: 16 (over y, x).
Axes of the slice: x: 4, y: 4, z: 4, core: 2. Of those that a mesh axis runs over, the one named last changes fastest.
Arguments:
- tokens: bfloat16 [512, 7168], P('local'), may hold values from -6 to 6
- cotangent: bfloat16 [512, 7168], P('local'), may hold values from -6 to 6
- gate_logits: float32 [512, 24], P('local'), may hold values from -8 to 8
- route_slot: int32 [512, 8], P('local'), may hold values from 0 to 31, all different within a row; in each aligned block of 32 rows (0 to 31, 32 to 63, ...) at most 16 rows name the same one
- slot_expert: int32 [32], replicated, may hold values from 0 to 23, as said below
- w_gate: bfloat16 [32, 7168, 1024], P('local', None, 'group')
- w_up: bfloat16 [32, 7168, 1024], P('local', None, 'group')
- w_down: bfloat16 [32, 1024, 7168], P('local', 'group'), as said below
Outputs:
- mixed: bfloat16 [512, 7168], P('local', 'group')
- grad_tokens: bfloat16 [512, 7168], P('local', 'group')
- grad_logits: float32 [512, 24], P('local')
- grad_gate: bfloat16 [32, 7168, 1024], P('local', None, 'group')
- grad_up: bfloat16 [32, 7168, 1024], P('local', None, 'group')
- grad_down: bfloat16 [32, 1024, 7168], P('local', 'group')
Inputs may be any that keep to these rules, and one draw needn't show every extreme that they name: `route_slot`: each token names 8 different slots. Of the 32 tokens of one index of local, at most 16 name one slot, a bound that some block reaches of them. `slot_expert`: the even slots hold 16 different experts, the odd slots the remaining ones, each on two odd slots: slot 2i + 1 and slot 2j + 1 hold the same expert where j = i plus or minus half the size of local (the one that stays in range). Every expert is held. `w_down`: two odd slots that hold the same expert have equal weights; entries have standard deviation 1024 ** -0.5.
All inputs are finite; a program needn't handle non-finite values.
Results may differ from a plain program's by a relative error of at most 0.019.
Values may be sent and summed in bfloat16 or wider, within the bound.
No kernel may reach another device: no remote copies, remote signals or barrier semaphores. Data moves between devices by JAX's collectives and lax.ppermute only.
A program may use at most 192 MiB of HBM per device.

v0:
```python
import jax
import jax.numpy as jnp
from jax import lax
from jax.sharding import PartitionSpec as P

ROUTE_SCALE = 2.5
CONTRACT_ONE = (((1,), (1,)), ((), ()))
CONTRACT_ZERO = (((0,), (0,)), ((), ()))


def swapped(block, axis, apart):
    count = lax.axis_size(axis)
    route = []
    for low in range(count):
        high = low | 1 << apart
        if high != low and high < count:
            route += [(low, high), (high, low)]
    return lax.ppermute(block, axis, route)


def gate_weights(logits, expert_ids, experts):
    match = expert_ids[:, :, None] == jnp.arange(experts, dtype=jnp.int32)[None, None, :]
    picked = jnp.sum(jnp.where(match, logits[:, None, :], 0.0), axis=2)
    sig = jax.nn.sigmoid(picked)
    return ROUTE_SCALE * sig / jnp.sum(sig, axis=1, keepdims=True)


def activations(rows_x, rows_g, w_g, w_u, w_d):
    first = jnp.dot(rows_x, w_g, preferred_element_type=jnp.float32)
    second = jnp.dot(rows_x, w_u, preferred_element_type=jnp.float32)
    sig = jax.nn.sigmoid(first)
    silu = first * sig
    hidden = (silu * second).astype(jnp.bfloat16)
    back = lax.dot_general(rows_g, w_d, CONTRACT_ONE, preferred_element_type=jnp.float32)
    d_first = (back * second * sig * (1.0 + first * (1.0 - sig))).astype(jnp.bfloat16)
    d_second = (back * silu).astype(jnp.bfloat16)
    return (hidden, d_first, d_second)


def weight_grads(rows_x, rows_g, hidden, d_first, d_second):
    own_gate = lax.dot_general(rows_x, d_first, CONTRACT_ZERO, preferred_element_type=jnp.float32)
    own_up = lax.dot_general(rows_x, d_second, CONTRACT_ZERO, preferred_element_type=jnp.float32)
    own_down = lax.dot_general(hidden, rows_g, CONTRACT_ZERO, preferred_element_type=jnp.float32)
    return (
        own_gate.astype(jnp.bfloat16),
        own_up.astype(jnp.bfloat16),
        own_down.astype(jnp.bfloat16),
    )


def slot_pass(rows_x, rows_g, w_g, w_u, w_d):
    hidden, d_first, d_second = activations(rows_x, rows_g, w_g, w_u, w_d)
    out_rows = jnp.dot(hidden, w_d, preferred_element_type=jnp.float32).astype(jnp.bfloat16)
    both = lax.dot_general(d_first, w_g, CONTRACT_ONE, preferred_element_type=jnp.float32)
    both = both + lax.dot_general(d_second, w_u, CONTRACT_ONE, preferred_element_type=jnp.float32)
    grad_rows = both.astype(jnp.bfloat16)
    return (out_rows, grad_rows, weight_grads(rows_x, rows_g, hidden, d_first, d_second))


def per_device(tokens, cotangent, gate_logits, route_slot, slot_expert, w_gate, w_up, w_down):
    tok = tokens.shape[0]
    width = tokens.shape[1]
    top = route_slot.shape[1]
    slots = slot_expert.shape[0]
    experts = gate_logits.shape[1]
    lines = lax.axis_size("local")
    cap = top * tok // lines
    match_slot = route_slot[:, :, None] == jnp.arange(slots, dtype=jnp.int32)[None, None, :]
    expert_ids = jnp.sum(jnp.where(match_slot, slot_expert[None, None, :], 0), axis=2)
    weights, pull_back = jax.vjp(lambda lg: gate_weights(lg, expert_ids, experts), gate_logits)
    scaled = (weights[:, :, None] * cotangent.astype(jnp.float32)[:, None, :]).astype(jnp.bfloat16)
    flat = route_slot.reshape(-1)
    onehot = (flat[:, None] == jnp.arange(slots, dtype=jnp.int32)[None, :]).astype(jnp.int32)
    rank = jnp.sum((jnp.cumsum(onehot, axis=0) - onehot) * onehot, axis=1)
    target = flat * cap + rank
    placer = (jnp.arange(slots * cap, dtype=jnp.int32)[:, None] == target[None, :]).astype(
        jnp.bfloat16
    )
    token_placer = jnp.sum(placer.reshape(slots * cap, tok, top), axis=2)
    x_buffer = jnp.dot(token_placer, tokens, preferred_element_type=jnp.float32).astype(
        jnp.bfloat16
    )
    g_buffer = jnp.dot(
        placer, scaled.reshape(tok * top, width), preferred_element_type=jnp.float32
    ).astype(jnp.bfloat16)
    x_buffer = x_buffer.reshape(lines, 2 * cap, width)
    g_buffer = g_buffer.reshape(lines, 2 * cap, width)
    got_x, got_g = (
        lax.all_to_all(x_buffer, "local", split_axis=0, concat_axis=0, tiled=True),
        lax.all_to_all(g_buffer, "local", split_axis=0, concat_axis=0, tiled=True),
    )
    got_x = got_x.reshape(lines, 2, cap, width)
    got_g = got_g.reshape(lines, 2, cap, width)
    rows_cold_x = got_x[:, 0].reshape(lines * cap, width)
    rows_cold_g = got_g[:, 0].reshape(lines * cap, width)
    rows_hot_x = got_x[:, 1].reshape(lines * cap, width)
    rows_hot_g = got_g[:, 1].reshape(lines * cap, width)
    out_cold, dx_cold, grads_cold = slot_pass(
        rows_cold_x, rows_cold_g, w_gate[0], w_up[0], w_down[0]
    )
    out_hot, dx_hot, grads_hot = slot_pass(rows_hot_x, rows_hot_g, w_gate[1], w_up[1], w_down[1])
    outs_back = jnp.stack(
        [out_cold.reshape(lines, cap, width), out_hot.reshape(lines, cap, width)], axis=1
    )
    dxs_back = jnp.stack(
        [dx_cold.reshape(lines, cap, width), dx_hot.reshape(lines, cap, width)], axis=1
    )
    outs_back = outs_back.reshape(lines, 2 * cap, width)
    dxs_back = dxs_back.reshape(lines, 2 * cap, width)
    home_out, home_dx = (
        lax.all_to_all(outs_back, "local", split_axis=0, concat_axis=0, tiled=True),
        lax.all_to_all(dxs_back, "local", split_axis=0, concat_axis=0, tiled=True),
    )
    home_out = home_out.reshape(slots * cap, width)
    home_dx = home_dx.reshape(slots * cap, width)
    gathered = lax.dot_general(placer, home_out, CONTRACT_ZERO, preferred_element_type=jnp.float32)
    gathered = gathered.reshape(tok, top, width)
    partial_out = jnp.sum(weights[:, :, None] * gathered, axis=1)
    partial_dx = lax.dot_general(
        token_placer, home_dx, CONTRACT_ZERO, preferred_element_type=jnp.float32
    )
    partial_dots = jnp.sum(cotangent.astype(jnp.float32)[:, None, :] * gathered, axis=2)
    mixed, grad_tokens = (
        lax.psum_scatter(
            partial_out.astype(jnp.bfloat16), "group", scatter_dimension=1, tiled=True
        ).astype(jnp.float32),
        lax.psum_scatter(
            partial_dx.astype(jnp.bfloat16), "group", scatter_dimension=1, tiled=True
        ).astype(jnp.float32),
    )
    gate_dots = lax.psum(partial_dots, "group")
    grad_logits = pull_back(gate_dots)[0]
    partner_bit = lax.axis_size("local").bit_length() - 2
    other = swapped((grads_hot[0], grads_hot[1], grads_hot[2]), "local", partner_bit)
    joined = [
        (mine.astype(jnp.float32) + theirs.astype(jnp.float32)).astype(jnp.bfloat16)
        for mine, theirs in zip(grads_hot, other)
    ]
    grad_gate = jnp.stack([grads_cold[0], joined[0]], axis=0)
    grad_up = jnp.stack([grads_cold[1], joined[1]], axis=0)
    grad_down = jnp.stack([grads_cold[2], joined[2]], axis=0)
    return (
        mixed.astype(jnp.bfloat16),
        grad_tokens.astype(jnp.bfloat16),
        grad_logits,
        grad_gate,
        grad_up,
        grad_down,
    )


def solution(mesh):
    return jax.shard_map(
        per_device,
        mesh=mesh,
        in_specs=(
            P("local", None),
            P("local", None),
            P("local", None),
            P("local", None),
            P(),
            P("local", None, "group"),
            P("local", None, "group"),
            P("local", "group", None),
        ),
        out_specs=(
            P("local", "group"),
            P("local", "group"),
            P("local", None),
            P("local", None, "group"),
            P("local", None, "group"),
            P("local", "group", None),
        ),
        check_vma=False,
    )
```

profile of v0, /device:TPU:0, one launch (start us, length us, event | category | flops | bytes accessed | tf_op | source)
XLA Modules:
  0.0 620.1 jit_solution(16297483419287537097)
XLA Ops:
  9.5 5.0 convolution_convert_fusion.1
  14.5 7.3 %all-to-all-start = ((bf16[16,32,7168]{2,1,0:T(8,128)(2,1)}), bf16[16,32,7168]{2,1,0:T(8,128)(2,1)}, u32[]{:S(2)}, u32[]{:S(2)}) async-start(bf16[16,32,7168]{2,1,0:T(8,128)(2,1)} %bitcast.142), calls=%async_computation | async-start | bytes 14680064 | tf_op jit(solution)/shard_map/all_to_all | solution.py:89
  22.9 5.2 convolution_convert_fusion
  28.1 102.3 %all-to-all-done = bf16[16,32,7168]{2,1,0:T(8,128)(2,1)} async-done(((bf16[16,32,7168]{2,1,0:T(8,128)(2,1)}), bf16[16,32,7168]{2,1,0:T(8,128)(2,1)}, u32[]{:S(2)}, u32[]{:S(2)}) %all-to-all-start) | async-done | bytes 7340064 | tf_op jit(solution)/shard_map/all_to_all | solution.py:89
  130.5 5.8 all-to-all-start.2
  136.3 3.8 fusion.60
  148.3 94.5 %all-to-all-done.2 = bf16[16,32,7168]{2,1,0:T(8,128)(2,1)} async-done(((bf16[16,32,7168]{2,1,0:T(8,128)(2,1)}), bf16[16,32,7168]{2,1,0:T(8,128)(2,1)}, u32[]{:S(2)}, u32[]{:S(2)}) %all-to-all-start.2) | async-done | bytes 7340064 | tf_op jit(solution)/shard_map/all_to_all | solution.py:90
  242.8 3.8 fusion.59
  258.0 3.8 pad_maximum_fusion.1
  261.8 4.9 all-to-all-start.3
  266.7 4.2 convolution_convert_fusion.4
  294.9 77.8 %all-to-all-done.3 = bf16[16,32,7168]{2,1,0:T(8,128)(2,1)} async-done(((bf16[16,32,7168]{2,1,0:T(8,128)(2,1)}), bf16[16,32,7168]{2,1,0:T(8,128)(2,1)}, u32[]{:S(2)}, u32[]{:S(2)}) %all-to-all-start.3) | async-done | bytes 7340064 | tf_op jit(solution)/shard_map/all_to_all | solution.py:112
  372.7 10.7 %all-to-all-start.1 = ((bf16[16,32,7168]{2,1,0:T(8,128)(2,1)}), bf16[16,32,7168]{2,1,0:T(8,128)(2,1)}, u32[]{:S(2)}, u32[]{:S(2)}) async-start(bf16[16,32,7168]{2,1,0:T(8,128)(2,1)} %bitcast.144), calls=%async_computation.1 | async-start | bytes 14680064 | tf_op jit(solution)/shard_map/all_to_all | solution.py:111
  383.8 58.0 %collective-permute-done.2 = bf16[128,7168]{1,0:T(8,128)(2,1)} collective-permute-done((bf16[128,7168]{1,0:T(8,128)(2,1)}, bf16[128,7168]{1,0:T(8,128)(2,1)}, u32[]{:S(2)}, u32[]{:S(2)}) %collective-permute-start.2) | collective-permute-done | bytes 1835040 | tf_op jit(solution)/shard_map/ppermute | solution.py:18
  446.5 44.4 %collective-permute-done.1 = bf16[7168,128]{1,0:T(8,128)(2,1)} collective-permute-done((bf16[7168,128]{1,0:T(8,128)(2,1)}, bf16[7168,128]{1,0:T(8,128)(2,1)}, u32[]{:S(2)}, u32[]{:S(2)}) %collective-permute-start.1) | collective-permute-done | bytes 1835040 | tf_op jit(solution)/shard_map/ppermute | solution.py:18
  490.9 3.7 fusion.10
  494.6 35.5 %collective-permute-done = bf16[7168,128]{1,0:T(8,128)(2,1)} collective-permute-done((bf16[7168,128]{1,0:T(8,128)(2,1)S(1)}, bf16[7168,128]{1,0:T(8,128)(2,1)}, u32[]{:S(2)}, u32[]{:S(2)}) %collective-permute-start) | collective-permute-done | bytes 1835040 | tf_op jit(solution)/shard_map/ppermute | solution.py:18
  533.4 4.5 convolution_convert_fusion.10
  539.8 3.7 pad_maximum_fusion.3
  543.5 4.1 all-to-all-done.1
  547.5 7.9 %multiply_reduce_fusion = (f32[32,8]{1,0:T(8,128)S(1)}, bf16[32,7168]{1,0:T(8,128)(2,1)S(1)}) fusion(f32[32,7168]{1,0:T(8,128)S(1)} %convert_element_type.121, f32[32,8]{1,0:T(8,128)S(1)} %copy.51, bf16[512,7168,1]{1,0,2:T(8,128)(2,1)} %bitcast.18, s32[256]{0:T(256)S(1)} %multiply_add_fusion.1), kind=kOutput, calls=%fused_computation.22 | convolution fusion | flops 1886289664 | bytes 8719360 | tf_op jit(solution)/shard_map/dot_general | solution.py:116
  557.4 3.7 pad_maximum_fusion.2
  561.2 14.0 %psum.7 = f32[32,8]{0,1:T(8,128)S(1)} all-reduce(f32[32,8]{0,1:T(8,128)S(1)} %copy.61), channel_id=1, replica_groups=mesh['group'=8,'local'=16] {'group'}, use_global_device_ids=true, to_apply=%region_11.12 | all-reduce | flops 256 | bytes 2048 | tf_op jit(solution)/shard_map/psum | solution.py:131
  578.8 32.8 %reduce-scatter.7.cloned.1.call-done = bf16[896,32]{1,0:T(8,128)(2,1)} async-done(((bf16[7168,32]{1,0:T(8,128)(2,1)}), bf16[896,32]{1,0:T(8,128)(2,1)}) %reduce-scatter.7.cloned.1.call-update) | async-done | bytes 57360
  (102 shorter events, 64.2 us)
Async XLA Ops:
  14.5 7.3 %copy-start.20 = (s32[32]{0:T(128)S(1)}, s32[32]{0:T(128)}, u32[]{:S(2)}) copy-start(s32[32]{0:T(128)} %param.12) | copy-start | bytes 388
  14.5 8.1 %copy-start.19 = (f32[32,24]{0,1:T(8,128)S(1)}, f32[32,24]{0,1:T(8,128)}, u32[]{:S(2)}) copy-start(f32[32,24]{0,1:T(8,128)} %param.10) | copy-start | bytes 9220
  14.5 8.3 %copy-start.18 = (bf16[32,7168]{1,0:T(8,128)(2,1)S(1)}, bf16[32,7168]{1,0:T(8,128)(2,1)}, u32[]{:S(2)}) copy-start(bf16[32,7168]{1,0:T(8,128)(2,1)} %param.9) | copy-start | bytes 1376260
  14.5 116.0 %all-to-all-start = ((bf16[16,32,7168]{2,1,0:T(8,128)(2,1)}), bf16[16,32,7168]{2,1,0:T(8,128)(2,1)}, u32[]{:S(2)}, u32[]{:S(2)}) async-start(bf16[16,32,7168]{2,1,0:T(8,128)(2,1)} %bitcast.142), calls=%async_computation | async-start | bytes 14680064 | tf_op jit(solution)/shard_map/all_to_all | solution.py:89
  130.5 112.4 %all-to-all-start.2 = ((bf16[16,32,7168]{2,1,0:T(8,128)(2,1)}), bf16[16,32,7168]{2,1,0:T(8,128)(2,1)}, u32[]{:S(2)}, u32[]{:S(2)}) async-start(bf16[16,32,7168]{2,1,0:T(8,128)(2,1)} %bitcast.143), calls=%async_computation.2 | async-start | bytes 14680064 | tf_op jit(solution)/shard_map/all_to_all | solution.py:90
  136.3 4.2 copy-start.12
  140.1 5.9 copy-start.4
  140.1 7.0 %copy-start.2 = (bf16[16,1,16,7168]{3,2,1,0:T(8,128)(2,1)}, bf16[16,1,16,7168]{3,2,1,0:T(8,128)(2,1)S(1)}, u32[]{:S(2)}) copy-start(bf16[16,1,16,7168]{3,2,1,0:T(8,128)(2,1)S(1)} %get-tuple-element.10) | copy-start | bytes 11010052
  140.1 4.8 copy-start.14
  242.8 4.2 copy-start.16
  246.6 5.9 copy-start.6
  246.6 5.9 copy-start.8
  246.6 4.8 copy-start.15
  261.8 111.0 %all-to-all-start.3 = ((bf16[16,32,7168]{2,1,0:T(8,128)(2,1)}), bf16[16,32,7168]{2,1,0:T(8,128)(2,1)}, u32[]{:S(2)}, u32[]{:S(2)}) async-start(bf16[16,32,7168]{2,1,0:T(8,128)(2,1)} %bitcast.145), calls=%async_computation.3 | async-start | bytes 14680064 | tf_op jit(solution)/shard_map/all_to_all | solution.py:112
  266.6 7.6 %copy-start.3 = (bf16[16,1,16,7168]{3,2,1,0:T(8,128)(2,1)S(1)}, bf16[16,1,16,7168]{3,2,1,0:T(8,128)(2,1)}, u32[]{:S(2)}) copy-start(bf16[16,1,16,7168]{3,2,1,0:T(8,128)(2,1)} %copy-done.2) | copy-start | bytes 11010052
  270.9 170.9 %collective-permute-start.2 = (bf16[128,7168]{1,0:T(8,128)(2,1)}, bf16[128,7168]{1,0:T(8,128)(2,1)}, u32[]{:S(2)}, u32[]{:S(2)}) collective-permute-start(bf16[128,7168]{1,0:T(8,128)(2,1)} %convolution_convert_fusion.4), channel_id=1, source_target_pairs={{0,8},{8,0},{1,9},{9,1},{2,10},{10,2},{3,11},{11,3},{4,12},{12,4},... | collective-permute-start | bytes 5505032 | tf_op jit(solution)/shard_map/ppermute | solution.py:18
  282.7 6.3 %copy-start.17 = (bf16[2,128,7168]{2,1,0:T(8,128)(2,1)S(1)}, bf16[2,128,7168]{2,1,0:T(8,128)(2,1)}, u32[]{:S(2)}) copy-start(bf16[2,128,7168]{2,1,0:T(8,128)(2,1)} %param.15) | copy-start | bytes 11010052
  285.5 205.4 %collective-permute-start.1 = (bf16[7168,128]{1,0:T(8,128)(2,1)}, bf16[7168,128]{1,0:T(8,128)(2,1)}, u32[]{:S(2)}, u32[]{:S(2)}) collective-permute-start(bf16[7168,128]{1,0:T(8,128)(2,1)} %convolution_convert_fusion.6), channel_id=1, source_target_pairs={{0,8},{8,0},{1,9},{9,1},{2,10},{10,2},{3,11},{11,3},{4,12},{12,4},... | collective-permute-start | bytes 5505032 | tf_op jit(solution)/shard_map/ppermute | solution.py:18
  285.6 244.5 %collective-permute-start = (bf16[7168,128]{1,0:T(8,128)(2,1)S(1)}, bf16[7168,128]{1,0:T(8,128)(2,1)}, u32[]{:S(2)}, u32[]{:S(2)}) collective-permute-start(bf16[7168,128]{1,0:T(8,128)(2,1)S(1)} %convolution_convert_fusion.8), channel_id=1, source_target_pairs={{0,8},{8,0},{1,9},{9,1},{2,10},{10,2},{3,11},{11,3},{4,12},{12,4},... | collective-permute-start | bytes 5505032 | tf_op jit(solution)/shard_map/ppermute | solution.py:18
  372.7 174.8 %all-to-all-start.1 = ((bf16[16,32,7168]{2,1,0:T(8,128)(2,1)}), bf16[16,32,7168]{2,1,0:T(8,128)(2,1)}, u32[]{:S(2)}, u32[]{:S(2)}) async-start(bf16[16,32,7168]{2,1,0:T(8,128)(2,1)} %bitcast.144), calls=%async_computation.1 | async-start | bytes 14680064 | tf_op jit(solution)/shard_map/all_to_all | solution.py:111
  383.5 193.7 %reduce-scatter.9.cloned.1.call-start = ((), (), s32[]{:S(2)}) async-start(), calls=%async_computation.7 | async-start | bytes 2064384
  383.8 60.5 %copy-start.11 = (bf16[1,128,7168]{2,1,0:T(8,128)(2,1)S(1)}, bf16[1,128,7168]{2,1,0:T(8,128)(2,1)}, u32[]{:S(2)}) copy-start(bf16[1,128,7168]{2,1,0:T(8,128)(2,1)} %fusion.4) | copy-start | bytes 5505028
  539.6 72.0 %reduce-scatter.7.cloned.1.call-start = ((), (), s32[]{:S(2)}) async-start(), calls=%async_computation.6 | async-start | bytes 2064384
  557.4 55.9 %copy-start.1 = (bf16[32,7168]{1,0:T(8,128)(2,1)S(1)}, bf16[32,7168]{1,0:T(8,128)(2,1)}, u32[]{:S(2)}) copy-start(bf16[32,7168]{1,0:T(8,128)(2,1)} %param.8) | copy-start | bytes 1376260
  (6 other events, 12.6 us)
Sparse Core Ops, SparseCore 0:
  539.7 37.4 reduce-scatter.8
  579.6 31.9 reduce-scatter.6
where the time goes:
time: 621 us; the launch traced here: 620 us
  waiting for transfers between devices  451 us (73%)
  matrix products  50.6 us (8%)
  starting transfers between devices  36 us (6%)
  other arithmetic  29 us (5%)
  local copies, waits for them, and re-layouts  25.2 us (4%)
  between operations  14.5 us (2%)
  blocking collectives  14 us (2%)
    ppermute x3, waiting for transfers between devices, swapped(): return lax.ppermute(block, axis, route)  138 us
    all_to_all x1, waiting for transfers between devices, per_device(): lax.all_to_all(x_buffer, 'local', split_axis=0, concat_axis=0, tiled=True)  102 us
    all_to_all x1, waiting for transfers between devices, per_device(): lax.all_to_all(g_buffer, 'local', split_axis=0, concat_axis=0, tiled=True)  94.5 us
    all_to_all x1, waiting for transfers between devices, per_device(): lax.all_to_all(dxs_back, 'local', split_axis=0, concat_axis=0, tiled=True)  77.8 us
    unnamed x4, waiting for transfers between devices  34.1 us
    unnamed x47, local copies, waits for them, and re-layouts  17 us
    psum x1, blocking collectives, per_device(): gate_dots = lax.psum(partial_dots, 'group')  14 us
  transfers between devices with their start and end apart: 9, of which 9 were waited for; matrix products, arithmetic and copies ran while one was open for 12% of the time, Pallas kernels for 0%

commit v1 on v0

--- a/solution.py
+++ b/solution.py
@@ -128,7 +128,7 @@
             partial_dx.astype(jnp.bfloat16), "group", scatter_dimension=1, tiled=True
         ).astype(jnp.float32),
     )
-    gate_dots = lax.psum(partial_dots, "group")
+    gate_dots = jnp.sum(lax.all_gather(partial_dots, "group"), axis=0)
     grad_logits = pull_back(gate_dots)[0]
     partner_bit = lax.axis_size("local").bit_length() - 2
     other = swapped((grads_hot[0], grads_hot[1], grads_hot[2]), "local", partner_bit)

time: 621 us -> 621 us (level)
    all_gather x0 -> x1, blocking collectives: none -> 14 us  [per_device(): gate_dots = jnp.sum(lax.all_gather(partial_dots, 'group'), axis=0)]
    psum x1 -> x0, blocking collectives: 14 us -> none  [per_device(): gate_dots = lax.psum(partial_dots, 'group')]
    unnamed x47 -> x48, local copies, waits for them, and re-layouts: 17 us -> 17 us
where the time goes in v1:
time: 621 us; the launch traced here: 620 us
  waiting for transfers between devices  451 us (73%)
  matrix products  50.6 us (8%)
  starting transfers between devices  36 us (6%)
  other arithmetic  29 us (5%)
  local copies, waits for them, and re-layouts  25.2 us (4%)
  between operations  14.5 us (2%)
  blocking collectives  14 us (2%)
    ppermute x3, waiting for transfers between devices, swapped(): return lax.ppermute(block, axis, route)  138 us
    all_to_all x1, waiting for transfers between devices, per_device(): lax.all_to_all(x_buffer, 'local', split_axis=0, concat_axis=0, tiled=True)  102 us
    all_to_all x1, waiting for transfers between devices, per_device(): lax.all_to_all(g_buffer, 'local', split_axis=0, concat_axis=0, tiled=True)  94.5 us
    all_to_all x1, waiting for transfers between devices, per_device(): lax.all_to_all(dxs_back, 'local', split_axis=0, concat_axis=0, tiled=True)  77.8 us
    unnamed x4, waiting for transfers between devices  34.1 us
    unnamed x48, local copies, waits for them, and re-layouts  17 us
    all_gather x1, blocking collectives, per_device(): gate_dots = jnp.sum(lax.all_gather(partial_dots, 'group'), axis=0)  14 us
  transfers between devices with their start and end apart: 9, of which 9 were waited for; matrix products, arithmetic and copies ran while one was open for 12% of the time, Pallas kernels for 0%

profile of v1, /device:TPU:0, one launch (start us, length us, event | category | flops | bytes accessed | tf_op | source)
XLA Modules:
  0.0 620.1 jit_solution(2913686992960729307)
XLA Ops:
  9.5 5.0 convolution_convert_fusion.1
  14.5 7.3 %all-to-all-start = ((bf16[16,32,7168]{2,1,0:T(8,128)(2,1)}), bf16[16,32,7168]{2,1,0:T(8,128)(2,1)}, u32[]{:S(2)}, u32[]{:S(2)}) async-start(bf16[16,32,7168]{2,1,0:T(8,128)(2,1)} %bitcast.143), calls=%async_computation | async-start | bytes 14680064 | tf_op jit(solution)/shard_map/all_to_all | solution.py:89
  22.9 5.2 convolution_convert_fusion
  28.1 102.3 %all-to-all-done = bf16[16,32,7168]{2,1,0:T(8,128)(2,1)} async-done(((bf16[16,32,7168]{2,1,0:T(8,128)(2,1)}), bf16[16,32,7168]{2,1,0:T(8,128)(2,1)}, u32[]{:S(2)}, u32[]{:S(2)}) %all-to-all-start) | async-done | bytes 7340064 | tf_op jit(solution)/shard_map/all_to_all | solution.py:89
  130.5 5.8 all-to-all-start.2
  136.3 3.8 fusion.60
  148.3 94.5 %all-to-all-done.2 = bf16[16,32,7168]{2,1,0:T(8,128)(2,1)} async-done(((bf16[16,32,7168]{2,1,0:T(8,128)(2,1)}), bf16[16,32,7168]{2,1,0:T(8,128)(2,1)}, u32[]{:S(2)}, u32[]{:S(2)}) %all-to-all-start.2) | async-done | bytes 7340064 | tf_op jit(solution)/shard_map/all_to_all | solution.py:90
  242.8 3.8 fusion.59
  258.0 3.8 pad_maximum_fusion.1
  261.8 4.9 all-to-all-start.3
  266.7 4.2 convolution_convert_fusion.4
  294.9 77.8 %all-to-all-done.3 = bf16[16,32,7168]{2,1,0:T(8,128)(2,1)} async-done(((bf16[16,32,7168]{2,1,0:T(8,128)(2,1)}), bf16[16,32,7168]{2,1,0:T(8,128)(2,1)}, u32[]{:S(2)}, u32[]{:S(2)}) %all-to-all-start.3) | async-done | bytes 7340064 | tf_op jit(solution)/shard_map/all_to_all | solution.py:112
  372.7 10.7 %all-to-all-start.1 = ((bf16[16,32,7168]{2,1,0:T(8,128)(2,1)}), bf16[16,32,7168]{2,1,0:T(8,128)(2,1)}, u32[]{:S(2)}, u32[]{:S(2)}) async-start(bf16[16,32,7168]{2,1,0:T(8,128)(2,1)} %bitcast.145), calls=%async_computation.1 | async-start | bytes 14680064 | tf_op jit(solution)/shard_map/all_to_all | solution.py:111
  383.8 58.0 %collective-permute-done.2 = bf16[128,7168]{1,0:T(8,128)(2,1)} collective-permute-done((bf16[128,7168]{1,0:T(8,128)(2,1)}, bf16[128,7168]{1,0:T(8,128)(2,1)}, u32[]{:S(2)}, u32[]{:S(2)}) %collective-permute-start.2) | collective-permute-done | bytes 1835040 | tf_op jit(solution)/shard_map/ppermute | solution.py:18
  446.5 44.4 %collective-permute-done.1 = bf16[7168,128]{1,0:T(8,128)(2,1)} collective-permute-done((bf16[7168,128]{1,0:T(8,128)(2,1)}, bf16[7168,128]{1,0:T(8,128)(2,1)}, u32[]{:S(2)}, u32[]{:S(2)}) %collective-permute-start.1) | collective-permute-done | bytes 1835040 | tf_op jit(solution)/shard_map/ppermute | solution.py:18
  490.9 3.7 fusion.10
  494.6 35.5 %collective-permute-done = bf16[7168,128]{1,0:T(8,128)(2,1)} collective-permute-done((bf16[7168,128]{1,0:T(8,128)(2,1)S(1)}, bf16[7168,128]{1,0:T(8,128)(2,1)}, u32[]{:S(2)}, u32[]{:S(2)}) %collective-permute-start) | collective-permute-done | bytes 1835040 | tf_op jit(solution)/shard_map/ppermute | solution.py:18
  533.4 4.5 convolution_convert_fusion.10
  539.8 3.7 pad_maximum_fusion.3
  543.5 4.1 all-to-all-done.1
  547.5 7.9 %multiply_reduce_fusion = (f32[32,8]{1,0:T(8,128)S(1)}, bf16[32,7168]{1,0:T(8,128)(2,1)S(1)}) fusion(f32[32,7168]{1,0:T(8,128)S(1)} %convert_element_type.121, f32[32,8]{1,0:T(8,128)S(1)} %copy.53, bf16[512,7168,1]{1,0,2:T(8,128)(2,1)} %bitcast.18, s32[256]{0:T(256)S(1)} %multiply_add_fusion.1), kind=kOutput, calls=%fused_computation.22 | convolution fusion | flops 1886289664 | bytes 8719360 | tf_op jit(solution)/shard_map/dot_general | solution.py:116
  557.4 3.7 pad_maximum_fusion.2
  561.2 14.0 %all-gather.1 = f32[8,32,8]{1,2,0:T(8,128)S(1)} all-gather(f32[1,32,8]{1,2,0:T(8,128)S(1)} %copy.63), channel_id=2, replica_groups=mesh['group'=8,'local'=16] {'group'}, dimensions={0}, use_global_device_ids=true | all-gather | bytes 9216 | tf_op jit(solution)/shard_map/all_gather | solution.py:131
  578.8 32.8 %reduce-scatter.7.cloned.1.call-done = bf16[896,32]{1,0:T(8,128)(2,1)} async-done(((bf16[7168,32]{1,0:T(8,128)(2,1)}), bf16[896,32]{1,0:T(8,128)(2,1)}) %reduce-scatter.7.cloned.1.call-update) | async-done | bytes 57360
  (103 shorter events, 64.1 us)
Async XLA Ops:
  14.5 7.3 %copy-start.20 = (s32[32]{0:T(128)S(1)}, s32[32]{0:T(128)}, u32[]{:S(2)}) copy-start(s32[32]{0:T(128)} %param.12) | copy-start | bytes 388
  14.5 8.1 %copy-start.19 = (f32[32,24]{0,1:T(8,128)S(1)}, f32[32,24]{0,1:T(8,128)}, u32[]{:S(2)}) copy-start(f32[32,24]{0,1:T(8,128)} %param.10) | copy-start | bytes 9220
  14.5 8.3 %copy-start.18 = (bf16[32,7168]{1,0:T(8,128)(2,1)S(1)}, bf16[32,7168]{1,0:T(8,128)(2,1)}, u32[]{:S(2)}) copy-start(bf16[32,7168]{1,0:T(8,128)(2,1)} %param.9) | copy-start | bytes 1376260
  14.5 116.0 %all-to-all-start = ((bf16[16,32,7168]{2,1,0:T(8,128)(2,1)}), bf16[16,32,7168]{2,1,0:T(8,128)(2,1)}, u32[]{:S(2)}, u32[]{:S(2)}) async-start(bf16[16,32,7168]{2,1,0:T(8,128)(2,1)} %bitcast.143), calls=%async_computation | async-start | bytes 14680064 | tf_op jit(solution)/shard_map/all_to_all | solution.py:89
  130.5 112.4 %all-to-all-start.2 = ((bf16[16,32,7168]{2,1,0:T(8,128)(2,1)}), bf16[16,32,7168]{2,1,0:T(8,128)(2,1)}, u32[]{:S(2)}, u32[]{:S(2)}) async-start(bf16[16,32,7168]{2,1,0:T(8,128)(2,1)} %bitcast.144), calls=%async_computation.2 | async-start | bytes 14680064 | tf_op jit(solution)/shard_map/all_to_all | solution.py:90
  136.3 4.2 copy-start.12
  140.1 5.9 copy-start.4
  140.1 7.0 %copy-start.2 = (bf16[16,1,16,7168]{3,2,1,0:T(8,128)(2,1)}, bf16[16,1,16,7168]{3,2,1,0:T(8,128)(2,1)S(1)}, u32[]{:S(2)}) copy-start(bf16[16,1,16,7168]{3,2,1,0:T(8,128)(2,1)S(1)} %get-tuple-element.10) | copy-start | bytes 11010052
  140.1 4.8 copy-start.14
  242.8 4.2 copy-start.16
  246.6 5.9 copy-start.6
  246.6 5.9 copy-start.8
  246.6 4.8 copy-start.15
  261.8 111.0 %all-to-all-start.3 = ((bf16[16,32,7168]{2,1,0:T(8,128)(2,1)}), bf16[16,32,7168]{2,1,0:T(8,128)(2,1)}, u32[]{:S(2)}, u32[]{:S(2)}) async-start(bf16[16,32,7168]{2,1,0:T(8,128)(2,1)} %bitcast.146), calls=%async_computation.3 | async-start | bytes 14680064 | tf_op jit(solution)/shard_map/all_to_all | solution.py:112
  266.6 7.6 %copy-start.3 = (bf16[16,1,16,7168]{3,2,1,0:T(8,128)(2,1)S(1)}, bf16[16,1,16,7168]{3,2,1,0:T(8,128)(2,1)}, u32[]{:S(2)}) copy-start(bf16[16,1,16,7168]{3,2,1,0:T(8,128)(2,1)} %copy-done.2) | copy-start | bytes 11010052
  270.9 170.9 %collective-permute-start.2 = (bf16[128,7168]{1,0:T(8,128)(2,1)}, bf16[128,7168]{1,0:T(8,128)(2,1)}, u32[]{:S(2)}, u32[]{:S(2)}) collective-permute-start(bf16[128,7168]{1,0:T(8,128)(2,1)} %convolution_convert_fusion.4), channel_id=1, source_target_pairs={{0,8},{8,0},{1,9},{9,1},{2,10},{10,2},{3,11},{11,3},{4,12},{12,4},... | collective-permute-start | bytes 5505032 | tf_op jit(solution)/shard_map/ppermute | solution.py:18
  282.7 6.3 %copy-start.17 = (bf16[2,128,7168]{2,1,0:T(8,128)(2,1)S(1)}, bf16[2,128,7168]{2,1,0:T(8,128)(2,1)}, u32[]{:S(2)}) copy-start(bf16[2,128,7168]{2,1,0:T(8,128)(2,1)} %param.15) | copy-start | bytes 11010052
  285.5 205.4 %collective-permute-start.1 = (bf16[7168,128]{1,0:T(8,128)(2,1)}, bf16[7168,128]{1,0:T(8,128)(2,1)}, u32[]{:S(2)}, u32[]{:S(2)}) collective-permute-start(bf16[7168,128]{1,0:T(8,128)(2,1)} %convolution_convert_fusion.6), channel_id=1, source_target_pairs={{0,8},{8,0},{1,9},{9,1},{2,10},{10,2},{3,11},{11,3},{4,12},{12,4},... | collective-permute-start | bytes 5505032 | tf_op jit(solution)/shard_map/ppermute | solution.py:18
  285.6 244.5 %collective-permute-start = (bf16[7168,128]{1,0:T(8,128)(2,1)S(1)}, bf16[7168,128]{1,0:T(8,128)(2,1)}, u32[]{:S(2)}, u32[]{:S(2)}) collective-permute-start(bf16[7168,128]{1,0:T(8,128)(2,1)S(1)} %convolution_convert_fusion.8), channel_id=1, source_target_pairs={{0,8},{8,0},{1,9},{9,1},{2,10},{10,2},{3,11},{11,3},{4,12},{12,4},... | collective-permute-start | bytes 5505032 | tf_op jit(solution)/shard_map/ppermute | solution.py:18
  372.7 174.8 %all-to-all-start.1 = ((bf16[16,32,7168]{2,1,0:T(8,128)(2,1)}), bf16[16,32,7168]{2,1,0:T(8,128)(2,1)}, u32[]{:S(2)}, u32[]{:S(2)}) async-start(bf16[16,32,7168]{2,1,0:T(8,128)(2,1)} %bitcast.145), calls=%async_computation.1 | async-start | bytes 14680064 | tf_op jit(solution)/shard_map/all_to_all | solution.py:111
  383.5 193.7 %reduce-scatter.9.cloned.1.call-start = ((), (), s32[]{:S(2)}) async-start(), calls=%async_computation.7 | async-start | bytes 2064384
  383.8 60.5 %copy-start.11 = (bf16[1,128,7168]{2,1,0:T(8,128)(2,1)S(1)}, bf16[1,128,7168]{2,1,0:T(8,128)(2,1)}, u32[]{:S(2)}) copy-start(bf16[1,128,7168]{2,1,0:T(8,128)(2,1)} %fusion.4) | copy-start | bytes 5505028
  539.6 72.0 %reduce-scatter.7.cloned.1.call-start = ((), (), s32[]{:S(2)}) async-start(), calls=%async_computation.6 | async-start | bytes 2064384
  557.4 55.9 %copy-start.1 = (bf16[32,7168]{1,0:T(8,128)(2,1)S(1)}, bf16[32,7168]{1,0:T(8,128)(2,1)}, u32[]{:S(2)}) copy-start(bf16[32,7168]{1,0:T(8,128)(2,1)} %param.8) | copy-start | bytes 1376260
  (6 other events, 12.6 us)
Sparse Core Ops, SparseCore 0:
  539.7 37.3 reduce-scatter.8
  579.5 32.0 reduce-scatter.6
